TPU v7x, 32 devices: a whole 2x2x4 slice. The times are simulated.
32 devices in a mesh: groups: 2 (over y), traj: 16 (over z, x, core).
Axes of the slice: x: 2, y: 2, z: 4, core: 2. Of those that a mesh axis runs over, the one named last changes fastest.
Arguments:
- trajectories: bfloat16 [16384, 192], P(('groups', 'traj')), parts along dimension 0
- landmark_index: int32 [1024], P(('groups', 'traj')), parts along dimension 0, may hold values from 0 to 8191, as said below
- start_vectors: float32 [16384, 32], P(('groups', 'traj')), parts along dimension 0, may hold values from -6 to 6
Outputs:
- embedding: float32 [16384, 32], P(('groups', 'traj')), parts along dimension 0
There are 2 independent parts, one for each index of `groups`. A program takes and returns all parts, laid end to end along the dimension named above; each array names one. Nothing has to cross between parts.
Inputs may be any that keep to these rules, and one draw needn't show every extreme that they name: `landmark_index`: entries b * 32 to (b + 1) * 32 - 1 are distinct rows of the range b * 512 to (b + 1) * 512 - 1, for every b.
All inputs are finite; a program needn't handle non-finite values.
Results may differ from a plain program's by a relative error of at most 0.0003.
Values may be sent and summed in bfloat16 or wider, within the bound.
A program may use at most 64 MiB of HBM per device.

v0:
```python
import math
import jax
import jax.numpy as jnp
from jax import lax
from jax.sharding import PartitionSpec as P

SWEEPS = 2
HIGH = lax.Precision.HIGHEST


def kernel_turned(rows, row_norms, lands):
    wide = lands.astype(jnp.float32)
    land_norms = jnp.sum(wide * wide, axis=1)
    cross = lax.dot_general(
        lands, rows, (((1,), (1,)), ((), ())), preferred_element_type=jnp.float32
    )
    dist = land_norms[:, None] + row_norms[None, :] - 2.0 * cross
    return jnp.exp(-dist * (2.0 / rows.shape[1]))


def column_fold(rows, row_norms, weighted):

    def fold(total, piece, start):
        count = piece.shape[0]
        width = math.gcd(count, 512)

        def step_block(j, acc):
            lands = lax.dynamic_slice_in_dim(piece, j * width, width, 0)
            block = kernel_turned(rows, row_norms, lands)
            part = jnp.dot(block, weighted, precision=HIGH, preferred_element_type=jnp.float32)
            return lax.dynamic_update_slice_in_dim(acc, part, j * width, 0)

        return lax.fori_loop(0, count // width, step_block, total)

    return fold


def row_fold(rows, row_norms, mixing):

    def fold(total, piece, start):
        count = piece.shape[0]
        width = math.gcd(count, 512)

        def step_block(j, acc):
            lands = lax.dynamic_slice_in_dim(piece, j * width, width, 0)
            block = kernel_turned(rows, row_norms, lands)
            mix = lax.dynamic_slice_in_dim(mixing, j * width, width, 0)
            return acc + lax.dot_general(
                block,
                mix,
                (((0,), (0,)), ((), ())),
                precision=HIGH,
                preferred_element_type=jnp.float32,
            )

        return lax.fori_loop(0, count // width, step_block, total)

    return fold


def over_columns(rows, row_norms, weighted, own_lands):
    total_lands = own_lands.shape[0] * lax.axis_size("traj")
    start = jnp.zeros((total_lands, weighted.shape[1]), jnp.float32)
    fold = column_fold(rows, row_norms, weighted)
    return fold(start, lax.all_gather(own_lands, "traj", axis=0, tiled=True), jnp.int32(0))


def over_rows(rows, row_norms, mixing, own_lands):
    start = jnp.zeros((rows.shape[0], mixing.shape[1]), jnp.float32)
    fold = row_fold(rows, row_norms, mixing)
    return fold(start, lax.all_gather(own_lands, "traj", axis=0, tiled=True), jnp.int32(0))


def orthonormal(block, gram):
    lower = jnp.linalg.cholesky(gram)
    return jax.scipy.linalg.solve_triangular(lower, block.T, lower=True).T


def orthonormal_upper(block, gram):
    return orthonormal(block[:, ::-1], gram[::-1, ::-1])[:, ::-1]


def landmark_reduce(partial_value, scale_all):
    total = lax.psum(partial_value, "traj")
    return total / scale_all


def local(trajectories, landmark_index, start_vectors):
    row_dev = trajectories.shape[0]
    wide_rows = trajectories.astype(jnp.float32)
    row_norms = jnp.sum(wide_rows * wide_rows, axis=1)
    local_index = landmark_index - lax.axis_index("traj") * row_dev
    own_lands = jnp.take(trajectories, local_index, axis=0)
    own_norms = jnp.take(row_norms, local_index, axis=0)
    total_lands = own_lands.shape[0] * lax.axis_size("traj")
    land_deg = over_rows(own_lands, own_norms, jnp.ones((total_lands, 1), jnp.float32), own_lands)
    deg_all = lax.all_gather(land_deg, "traj", axis=0, tiled=True)
    col_part = over_columns(trajectories, row_norms, jnp.ones((row_dev, 1), jnp.float32), own_lands)
    ratio = landmark_reduce(col_part, deg_all)
    degree = over_rows(trajectories, row_norms, ratio, own_lands)
    dinv = lax.rsqrt(degree)
    vectors = start_vectors
    gram_part = None
    for sweep in range(SWEEPS):
        if gram_part is not None:
            gram = lax.psum(gram_part, "traj")
            vectors = orthonormal_upper(vectors, gram)
        partial_value = over_columns(trajectories, row_norms, dinv * vectors, own_lands)
        scaled = landmark_reduce(partial_value, deg_all)
        vectors = dinv * over_rows(trajectories, row_norms, scaled, own_lands)
        gram_part = jnp.dot(vectors.T, vectors, precision=HIGH, preferred_element_type=jnp.float32)
    gram = lax.psum(gram_part, "traj")
    vectors = orthonormal(vectors, gram)
    return math.sqrt(row_dev * lax.axis_size("traj")) * vectors


def solution(mesh):
    return jax.shard_map(
        local,
        mesh=mesh,
        in_specs=(P(("groups", "traj"), None), P(("groups", "traj")), P(("groups", "traj"), None)),
        out_specs=P(("groups", "traj"), None),
        check_vma=False,
    )
```

profile of v0, /device:TPU:0, one launch (start us, length us, event | category | flops | bytes accessed | tf_op | source)
XLA Modules:
  0.0 389.3 jit_solution(15879041102556417802)
XLA Ops:
  6.5 0.0 copy-start
  6.5 0.0 all-reduce.5.cloned.1.call-start
  6.5 1.1 multiply_reduce_fusion.1
  7.6 0.0 copy-done
  7.6 0.1 copy.9
  7.7 0.0 copy-start.2
  7.8 0.6 copy-done.2
  8.4 0.7 gather_fusion.1
  9.1 0.6 gather_fusion
  9.8 0.1 broadcast_select_fusion
  9.8 23.8 %all_gather.4 = bf16[512,192]{1,0:T(8,128)(2,1)S(1)} all-gather(bf16[32,192]{1,0:T(8,128)(2,1)S(1)} %broadcast_select_fusion), channel_id=1, replica_groups=mesh['groups'=2,'traj'=16] {'traj'}, dimensions={0}, use_global_device_ids=true | all-gather | bytes 208896 | tf_op jit(solution)/shard_map/all_gather | solution.py:71
  33.6 0.1 multiply_reduce_fusion
  33.8 0.4 fusion.3
  34.1 0.2 fusion.7
  34.4 0.3 convolution_bitcast_fusion.2
  34.6 0.0 copy-start.3
  34.6 1.0 convolution_bitcast_fusion.1
  35.6 0.0 copy-done.3
  35.6 0.6 dynamic-slice
  36.9 0.2 dynamic-update-slice.2
  37.1 29.8 %all-reduce.1 = (f32[512,1]{0,1:T(1,128)S(1)}, f32[512]{0:T(512)S(1)}) all-reduce(f32[512,1]{0,1:T(1,128)S(1)} %convolution_bitcast_fusion.1, f32[512]{0:T(512)S(1)} %dynamic-update-slice.2), channel_id=1, replica_groups=mesh['groups'=2,'traj'=16] {'traj'}, use_global_device_ids=true, to_apply=%region_2.3 | all-reduce | flops 1024 | bytes 8192 | tf_op jit(solution)/shard_map/psum | solution.py:84
  66.9 0.0 copy-start.1
  66.9 0.7 fusion.29
  67.6 0.2 copy-done.1
  67.8 1.7 fusion.17
  69.4 0.0 all-reduce.5.cloned.1.call-update
  69.5 0.0 all-reduce.7.cloned.1.call-start
  69.5 86.2 %all-reduce.5.cloned.1.call-done = f32[512,32]{1,0:T(8,128)} async-done(((f32[512,32]{1,0:T(8,128)}), f32[512,32]{1,0:T(8,128)}) %all-reduce.5.cloned.1.call-update) | async-done | bytes 65552 | tf_op jit(solution)/shard_map/psum | solution.py:84
  155.7 1.7 convolution_multiply_fusion.4
  157.4 0.2 fusion.35
  157.7 0.1 rev.10
  157.8 0.1 rev.9
  157.8 60.0 %psum.37 = f32[32,32]{0,1:T(8,128)S(1)} all-reduce(f32[32,32]{0,1:T(8,128)S(1)} %rev.9), channel_id=1, replica_groups=mesh['groups'=2,'traj'=16] {'traj'}, use_global_device_ids=true, to_apply=%region_4.5 | all-reduce | flops 1024 | bytes 8192 | tf_op jit(solution)/shard_map/psum | solution.py:106
  217.8 0.1 copy.11
  217.9 2.9 cholesky.44
  220.9 0.6 compare_reduce_fusion.1
  221.5 0.7 fusion.21
  222.2 2.5 custom-call.6
  224.6 0.3 convolution_bitcast_fusion
  224.9 0.1 rev.11
  225.0 1.7 fusion.15
  226.7 0.0 all-reduce.7.cloned.1.call-update
  226.7 86.2 %all-reduce.7.cloned.1.call-done = f32[512,32]{1,0:T(8,128)} async-done(((f32[512,32]{1,0:T(8,128)}), f32[512,32]{1,0:T(8,128)}) %all-reduce.7.cloned.1.call-update) | async-done | bytes 65552 | tf_op jit(solution)/shard_map/psum | solution.py:84
  312.9 1.7 convolution_multiply_fusion.3
  314.6 0.2 fusion.36
  314.8 60.0 %psum.39 = f32[32,32]{0,1:T(8,128)S(1)} all-reduce(f32[32,32]{0,1:T(8,128)S(1)} %fusion.36), channel_id=1, replica_groups=mesh['groups'=2,'traj'=16] {'traj'}, use_global_device_ids=true, to_apply=%region_8.11 | all-reduce | flops 1024 | bytes 8192 | tf_op jit(solution)/shard_map/psum | solution.py:112
  374.8 0.1 copy.13
  374.9 2.9 cholesky.55
  377.8 0.6 compare_reduce_fusion
  378.5 0.7 fusion.22
  379.1 2.4 custom-call.7
  381.6 0.9 fusion.8
  (9 shorter events, 0.1 us)
Async XLA Ops:
  6.5 1.1 copy-start
  6.5 149.2 %all-reduce.5.cloned.1.call-start = ((), (), s32[]{:S(2)}) async-start(), calls=%async_computation | async-start | bytes 524288 | tf_op jit(solution)/shard_map/psum | solution.py:84
  7.7 0.7 copy-start.2
  34.6 1.0 copy-start.3
  66.9 0.8 copy-start.1
  69.5 243.4 %all-reduce.7.cloned.1.call-start = ((), (), s32[]{:S(2)}) async-start(), calls=%async_computation.1 | async-start | bytes 524288 | tf_op jit(solution)/shard_map/psum | solution.py:84
Sparse Core Ops, SparseCore 0:
  69.6 86.0 all-reduce.4
  226.8 85.9 all-reduce.6
where the time goes:
time: 390 us; the launch traced here: 389 us
  blocking collectives  174 us (45%)
  waiting for transfers between devices  172 us (44%)
  other arithmetic  14.7 us (4%)
  between operations  14.2 us (4%)
  matrix products  10.9 us (3%)
    psum x2, waiting for transfers between devices, landmark_reduce(): total = lax.psum(partial_value, 'traj')  172 us
    psum x2, blocking collectives, local(): gram = lax.psum(gram_part, 'traj')  120 us
    psum x1, blocking collectives, landmark_reduce(): total = lax.psum(partial_value, 'traj')  29.8 us
    all_gather x1, blocking collectives, over_rows(): lax.all_gather(own_lands, 'traj', axis=0, tiled=True)  23.8 us
  transfers between devices with their start and end apart: 2, of which 2 were waited for; matrix products, arithmetic and copies ran while one was open for 0% of the time, Pallas kernels for 0%

commit v1 on v0

--- a/solution.py
+++ b/solution.py
@@ -81,7 +81,8 @@
 
 
 def landmark_reduce(partial_value, scale_all):
-    total = lax.psum(partial_value, "traj")
+    leaf_make = lambda content: lax.all_gather(content, "traj").sum(axis=0)
+    total = leaf_make(partial_value)
     return total / scale_all
 
 

time: 390 us -> 308 us (0.79)
  waiting for transfers between devices: 172 us -> 72.2 us
  blocking collectives: 174 us -> 190 us
  local copies, waits for them, and re-layouts: 3.58 us -> 7.74 us
    psum x2 -> x0, waiting for transfers between devices: 172 us -> none  [landmark_reduce(): total = lax.psum(partial_value, 'traj')]
    all_gather x0 -> x2, waiting for transfers between devices: none -> 72.2 us  [landmark_reduce(): leaf_make = lambda content: lax.all_gather(content, 'traj').sum(axis=0)]
    unnamed x0 -> x1, blocking collectives: none -> 29.8 us
    psum x1 -> x0, blocking collectives: 29.8 us -> none  [landmark_reduce(): total = lax.psum(partial_value, 'traj')]
    all_gather x0 -> x1, blocking collectives: none -> 17.2 us  [landmark_reduce(): leaf_make = lambda content: lax.all_gather(content, 'traj').sum(axis=0)]
    unnamed x12 -> x14, local copies, waits for them, and re-layouts: 1.81 us -> 5.97 us
where the time goes in v1:
time: 308 us
  blocking collectives  190 us (62%)
  waiting for transfers between devices  72.2 us (23%)
  other arithmetic  15.1 us (5%)
  between operations  14.2 us (5%)
  matrix products  8.79 us (3%)
  local copies, waits for them, and re-layouts  7.74 us (3%)
    psum x2, blocking collectives, local(): gram = lax.psum(gram_part, 'traj')  119 us
    all_gather x2, waiting for transfers between devices, landmark_reduce(): leaf_make = lambda content: lax.all_gather(content, 'traj').sum(axis=0)  72.2 us
    unnamed x1, blocking collectives  29.8 us
    all_gather x1, blocking collectives, over_rows(): lax.all_gather(own_lands, 'traj', axis=0, tiled=True)  23.8 us
    all_gather x1, blocking collectives, landmark_reduce(): leaf_make = lambda content: lax.all_gather(content, 'traj').sum(axis=0)  17.2 us
    another operation x6, other arithmetic, orthonormal(): lower = jnp.linalg.cholesky(gram)  7.19 us
    another operation x4, other arithmetic, orthonormal(): return jax.scipy.linalg.solve_triangular(lower, block.T, lower=True).T  6.2 us
  transfers between devices with their start and end apart: 2, of which 2 were waited for; matrix products, arithmetic and copies ran while one was open for 0% of the time, Pallas kernels for 0%

profile of v1, /device:TPU:0, one launch (start us, length us, event | category | flops | bytes accessed | tf_op | source)
XLA Modules:
  0.0 308.1 jit_solution(3951639262392159583)
XLA Ops:
  6.5 0.0 copy-start
  6.5 0.0 all-gather.8.cloned.1.call-start
  6.5 1.1 multiply_reduce_fusion.1
  7.6 0.0 copy-done
  7.6 0.1 copy.14
  7.7 0.0 copy-start.2
  7.8 0.6 copy-done.2
  8.4 0.7 gather_fusion.1
  9.1 0.6 gather_fusion
  9.8 0.1 broadcast_select_fusion
  9.8 23.8 %all_gather.30 = bf16[512,192]{1,0:T(8,128)(2,1)S(1)} all-gather(bf16[32,192]{1,0:T(8,128)(2,1)S(1)} %broadcast_select_fusion), channel_id=1, replica_groups=mesh['groups'=2,'traj'=16] {'traj'}, dimensions={0}, use_global_device_ids=true | all-gather | bytes 208896 | tf_op jit(solution)/shard_map/all_gather | solution.py:71
  33.6 0.1 multiply_reduce_fusion
  33.8 0.4 fusion.3
  34.1 0.2 fusion.8
  34.3 0.0 copy-start.3
  34.4 0.1 convolution_bitcast_fusion.2
  34.5 0.5 copy-done.3
  35.0 0.6 dynamic-slice
  36.2 0.2 dynamic-update-slice.2
  36.5 29.8 %all-reduce = f32[512]{0:T(512)S(1)} all-reduce(f32[512]{0:T(512)S(1)} %dynamic-update-slice.2), channel_id=3, replica_groups=mesh['groups'=2,'traj'=16] {'traj'}, use_global_device_ids=true, to_apply=%add | all-reduce | flops 512 | bytes 4096
  66.3 1.0 convolution_bitcast_fusion.1
  67.3 17.2 %all-gather.4 = f32[16,1,512]{2,1,0:T(1,128)S(1)} all-gather(f32[1,1,512]{2,1,0:T(1,128)S(1)} %convolution_bitcast_fusion.1), channel_id=2, replica_groups=mesh['groups'=2,'traj'=16] {'traj'}, dimensions={0}, use_global_device_ids=true | all-gather | bytes 34816 | tf_op jit(solution)/shard_map/all_gather | solution.py:84
  84.5 0.0 copy-start.1
  84.5 0.6 fusion.33
  85.2 0.2 copy-done.1
  85.4 1.7 fusion.15
  87.1 0.0 all-gather.8.cloned.1.call-update
  87.1 0.0 all-gather.10.cloned.1.call-start
  87.2 36.8 %all-gather.8.cloned.1.call-done = f32[8192,32]{0,1:T(8,128)} async-done(((f32[512,32]{0,1:T(8,128)}), f32[8192,32]{0,1:T(8,128)}) %all-gather.8.cloned.1.call-update) | async-done | bytes 1048592 | tf_op jit(solution)/shard_map/all_gather | solution.py:84
  124.0 1.8 copy.21
  125.8 0.2 bitcast_reduce_fusion.1
  126.0 0.7 convolution_multiply_fusion.3
  126.7 0.2 fusion.34
  126.9 0.1 rev.10
  127.0 0.1 rev.9
  127.1 59.6 %psum.14 = f32[32,32]{0,1:T(8,128)S(1)} all-reduce(f32[32,32]{0,1:T(8,128)S(1)} %rev.9), channel_id=1, replica_groups=mesh['groups'=2,'traj'=16] {'traj'}, use_global_device_ids=true, to_apply=%region_4.5 | all-reduce | flops 1024 | bytes 8192 | tf_op jit(solution)/shard_map/psum | solution.py:107
  186.7 0.1 copy.16
  186.8 2.9 cholesky.44
  189.8 0.6 compare_reduce_fusion.1
  190.4 0.7 fusion.21
  191.1 2.5 custom-call.6
  193.5 0.3 convolution_bitcast_fusion
  193.8 0.1 rev.11
  193.9 1.7 fusion.12
  195.6 0.0 all-gather.10.cloned.1.call-update
  195.6 35.4 %all-gather.10.cloned.1.call-done = f32[8192,32]{0,1:T(8,128)} async-done(((f32[512,32]{0,1:T(8,128)}), f32[8192,32]{0,1:T(8,128)}) %all-gather.10.cloned.1.call-update) | async-done | bytes 1048592 | tf_op jit(solution)/shard_map/all_gather | solution.py:84
  231.0 1.8 copy.22
  232.8 0.2 bitcast_reduce_fusion
  233.0 0.7 convolution_multiply_fusion.2
  233.7 0.2 fusion.35
  233.9 59.6 %psum.15 = f32[32,32]{0,1:T(8,128)S(1)} all-reduce(f32[32,32]{0,1:T(8,128)S(1)} %fusion.35), channel_id=1, replica_groups=mesh['groups'=2,'traj'=16] {'traj'}, use_global_device_ids=true, to_apply=%region_8.11 | all-reduce | flops 1024 | bytes 8192 | tf_op jit(solution)/shard_map/psum | solution.py:113
  293.6 0.1 copy.18
  293.6 2.9 cholesky.55
  296.6 0.6 compare_reduce_fusion
  297.2 0.7 fusion.22
  297.9 2.4 custom-call.7
  300.3 0.9 fusion.4
  (11 shorter events, 0.1 us)
Async XLA Ops:
  6.5 1.1 copy-start
  6.5 117.4 %all-gather.8.cloned.1.call-start = ((), (), s32[]{:S(2)}) async-start(), calls=%async_computation | async-start | bytes 1114112 | tf_op jit(solution)/shard_map/all_gather | solution.py:84
  7.7 0.7 copy-start.2
  34.3 0.7 copy-start.3
  84.5 0.8 copy-start.1
  87.1 143.9 %all-gather.10.cloned.1.call-start = ((), (), s32[]{:S(2)}) async-start(), calls=%async_computation.1 | async-start | bytes 1114112 | tf_op jit(solution)/shard_map/all_gather | solution.py:84
Sparse Core Ops, SparseCore 0:
  87.2 36.6 all-gather.7
  195.7 35.2 all-gather.9
